TPU v7x, 512 devices: a whole 4x8x8 slice. The times are simulated.
512 devices in a mesh: group: 8 (over y), dev: 64 (over x, z, core).
Axes of the slice: x: 4, y: 8, z: 8, core: 2. Of those that a mesh axis runs over, the one named last changes fastest.
Arguments:
- coords: float32 [3, 32, 256, 128], P(None, 'group', 'dev'), as said below
- charges: float32 [8, 32, 256, 128], P(None, 'group', 'dev'), may hold values from -6 to 6
- leaf_order: int32 [32, 256, 128], P('group', 'dev'), may hold values from 0 to 2047, as said below
- near_list: int32 [27, 32, 256, 4], P(None, 'group', 'dev'), may hold values from -1 to 32767, as said below
- far_list: int32 [138, 32, 256, 4], P(None, 'group', 'dev'), may hold values from -1 to 32767, as said below
- coarse_list: int32 [32, 16, 128, 2], P(None, 'group', 'dev'), may hold values from -1 to 4095, as said below
Outputs:
- potential: float32 [8, 32, 256, 128], P(None, 'group', 'dev')
Inputs may be any that keep to these rules, and one draw needn't show every extreme that they name: `leaf_order`: within each block of 4 x 4 rows every position of the block appears once. `coords`: A point of leaf box (i, j, k) lies within 0.75 of (i + 0.5, j + 0.5, k + 0.5) in every coordinate. `near_list`: -1 marks an empty slot; other entries are distinct box numbers (i * 256 + j) * 4 + k at most one box away in each dimension, the box itself among them. `far_list`: -1 marks an empty slot; other entries are distinct box numbers at most three boxes away in each dimension, none of them in the box's near_list. `coarse_list`: -1 marks an empty slot; other entries are distinct parent numbers (i * 128 + j) * 2 + k at most two parents away in each dimension.
All inputs are finite; a program needn't handle non-finite values.
Results may differ from a plain program's by a relative error of at most 0.0033.
Values may be sent and summed in bfloat16 or wider, within the bound.
A program may use at most 192 MiB of HBM per device.

v0:
```python
import functools
import math

import jax
import jax.numpy as jnp
import ml_dtypes
import numpy as np
from jax import lax
from jax.experimental import pallas as pl
from jax.experimental.pallas import tpu as pltpu
from jax.sharding import PartitionSpec as P

MESH = pl.DeviceIdType.MESH
BF = jnp.bfloat16
F32 = jnp.float32

ORDER = 4
LENGTH_SCALE = 2.5
AMPLITUDE = 0.025
SHORT_SCALE = 0.5
SHORT_WEIGHT = 0.1
NUGGET = 0.5
LEAF_HALF = 0.75
PARENT_HALF = 1.25

B = 4
PTS = 32
WIDTH = B * PTS
RHS = 8
RANK = ORDER**3

KAPPA = math.log2(math.e) / LENGTH_SCALE**2
SCALE = math.sqrt(2.0 * KAPPA)
RATIO = (LENGTH_SCALE / SHORT_SCALE) ** 2
LOG_LONG = math.log2(AMPLITUDE)
LOG_SHORT = math.log2(SHORT_WEIGHT)
PENALTY = -1024.0

NODES = np.cos((2.0 * np.arange(ORDER) + 1.0) * (math.pi / (2.0 * ORDER)))
NEIGHBOURS = [(i, j) for i in (-1, 0, 1) for j in (-1, 0, 1) if (i, j) != (0, 0)]


def lagrange_np(values):
    out = []
    for a in range(ORDER):
        col = np.ones_like(values)
        for b in range(ORDER):
            if b != a:
                col = col * (values - NODES[b]) / (NODES[a] - NODES[b])
        out.append(col)
    return np.stack(out, axis=-1)


def coupling_np(half, cell, reach):
    offsets = np.arange(-reach, reach + 1) * cell
    gap = half * NODES[None, :, None] - half * NODES[None, None, :] - offsets[:, None, None]
    total = 0.0
    for amp, scale in ((AMPLITUDE, LENGTH_SCALE), (SHORT_WEIGHT, SHORT_SCALE)):
        f = np.exp(-gap * gap / scale**2)
        total = total + amp * np.einsum("xad,ybe,zcf->xyzabcdef", f, f, f)
    n = 2 * reach + 1
    return total.reshape(n, n, n, RANK, RANK)


def leaf_weights():
    table = coupling_np(LEAF_HALF, 1.0, 3)
    w = np.zeros((49, B, RANK, B, RANK))
    for zs in range(B):
        for zt in range(B):
            w[:, zs, :, zt, :] = table[:, :, zs - zt + 3].reshape(49, RANK, RANK).transpose(0, 2, 1)
    return w.reshape(49 * B * RANK, B * RANK).astype(ml_dtypes.bfloat16)


def parent_weights():
    table = coupling_np(PARENT_HALF, 2.0, 2)
    w = np.zeros((26, 2, RANK, 2, RANK))
    for zs in range(2):
        for zt in range(2):
            w[:25, zs, :, zt, :] = table[:, :, zs - zt + 2].reshape(25, RANK, RANK).transpose(0, 2, 1)
    return w.reshape(26 * 2 * RANK, 2 * RANK).astype(ml_dtypes.bfloat16)


def transfer_weights():
    shifts = np.array([-0.5, 0.5])
    f = lagrange_np((shifts[:, None] + LEAF_HALF * NODES[None, :]) / PARENT_HALF)
    t = np.einsum("xad,ybe,zcf->xyzabcdef", f, f, f).reshape(2, 2, 2, RANK, RANK)
    up = np.zeros((2, 2, B, RANK, 2, RANK))
    for z in range(B):
        up[:, :, z, :, z // 2, :] = t[:, :, z % 2]
    up = up.reshape(4, B * RANK, 2 * RANK)
    return (
        up.reshape(4 * B * RANK, 2 * RANK).astype(ml_dtypes.bfloat16),
        up.transpose(2, 0, 1).reshape(2 * RANK, 4 * B * RANK).astype(ml_dtypes.bfloat16),
    )


def iota(shape, dim):
    return lax.broadcasted_iota(jnp.int32, shape, dim)


def dot_nt(a, b):
    return lax.dot_general(a, b, (((1,), (1,)), ((), ())), preferred_element_type=F32)


def split2(v):
    hi = v.astype(BF).astype(F32)
    return hi, (v - hi).astype(BF).astype(F32)


def prep_kernel(coords_ref, charges_ref, order_ref, up_ref, cs_ref, np_ref, mb_ref, pm_ref, bb_ref):
    gx = lax.axis_index("group")
    gy = lax.axis_index("dev")
    cen_x = (B * gx + 2).astype(F32)
    cen_y = (B * gy + 2).astype(F32)
    row8 = iota((8, WIDTH), 0)
    lane8 = iota((8, WIDTH), 1)
    lane_box = lane8 // PTS
    centre = jnp.where(row8 == 0, cen_x, jnp.where(row8 == 1, cen_y, 2.0))
    sources = []
    for c in range(16):
        q = charges_ref[:, c // B, c % B, :]
        xyz = coords_ref[:, c // B, c % B, :]
        xyz = jnp.concatenate([xyz, jnp.zeros((5, WIDTH), F32)], axis=0) - jnp.where(
            row8 < 3, centre, 0.0
        )
        sources.append((q, xyz))
    moments = []
    for c in range(16):
        x, y = c // B, c % B
        order = jnp.broadcast_to(order_ref[x, y : y + 1, :], (8, WIDTH))
        hi = order // WIDTH
        lo = order % WIDTH
        q = jnp.zeros((8, WIDTH), F32)
        xyz = jnp.zeros((8, WIDTH), F32)
        for k in range(16):
            here = hi == k
            q = jnp.where(here, jnp.take_along_axis(sources[k][0], lo, axis=1), q)
            xyz = jnp.where(here, jnp.take_along_axis(sources[k][1], lo, axis=1), xyz)
        cs_ref[c] = q
        q_low = q.astype(BF)
        hi2, lo2 = split2(xyz * SCALE)
        lo3 = jnp.concatenate([jnp.zeros((3, WIDTH), F32), lo2[0:5]], axis=0)
        feat = jnp.where(row8 < 3, hi2, lo3)
        np_ref[x, y] = jnp.concatenate([feat, q_low.astype(F32)], axis=0).astype(BF)

        box_centre = jnp.where(
            row8 == 0, x - 1.5, jnp.where(row8 == 1, y - 1.5, lane_box.astype(F32) - 1.5)
        )
        u = (xyz - box_centre) * (1.0 / LEAF_HALF)
        diffs = [u - float(NODES[k]) for k in range(ORDER)]
        polys = []
        for a in range(ORDER):
            denom = 1.0
            poly = None
            for b in range(ORDER):
                if b != a:
                    denom *= float(NODES[a] - NODES[b])
                    poly = diffs[b] if poly is None else poly * diffs[b]
            polys.append(poly * (1.0 / denom))

        def spread(k, d):
            return jnp.broadcast_to(polys[k][d : d + 1, :], (8, WIDTH))

        r4 = row8 % 4
        z8 = jnp.where(
            r4 < 2,
            jnp.where(r4 == 0, spread(0, 2), spread(1, 2)),
            jnp.where(r4 == 2, spread(2, 2), spread(3, 2)),
        )
        yz = [jnp.where(row8 < 4, spread(2 * j, 1), spread(2 * j + 1, 1)) * z8 for j in range(2)]
        basis = jnp.concatenate([spread(a, 0) * yz[j] for a in range(ORDER) for j in range(2)], axis=0)
        lane64 = iota((RANK, WIDTH), 1) // PTS
        wide = jnp.concatenate([jnp.where(lane64 == z, basis, 0.0) for z in range(B)], axis=0).astype(BF)
        bb_ref[c] = wide
        m = dot_nt(q_low, wide).astype(BF)
        moments.append(m)
        m32 = m.astype(F32)
        mb_ref[x, y] = jnp.concatenate([m32[:, :128], m32[:, 128:]], axis=0).astype(BF)
    for px in range(2):
        rows = []
        for py in range(2):
            kids = [moments[(2 * px + sx) * B + 2 * py + sy].astype(F32) for sx in range(2) for sy in range(2)]
            rows.append(jnp.concatenate(kids, axis=1))
        lhs = jnp.concatenate(rows, axis=0).astype(BF)
        pm_ref[px] = jnp.dot(lhs, up_ref[...], preferred_element_type=F32).astype(BF)


def cut(side, size, width):
    if side == 0:
        return slice(0, size), slice(width, width + size)
    if side > 0:
        return slice(size - width, size), slice(0, width)
    return slice(0, width), slice(width + size, 2 * width + size)


def exchange_kernel(count_g, count_d, np_in, mb_in, pm_in, np_out, mb_out, pm_out, send, recv, local):
    g = lax.axis_index("group")
    d = lax.axis_index("dev")

    def there(i, j):
        return (lax.rem(g + i + count_g, count_g), lax.rem(d + j + count_d, count_d))

    barrier = pltpu.get_barrier_semaphore()
    for i, j in NEIGHBOURS:
        pl.semaphore_signal(barrier, inc=1, device_id=there(i, j), device_id_type=MESH)
    pl.semaphore_wait(barrier, len(NEIGHBOURS))

    def ds(s):
        return pl.ds(s.start, s.stop - s.start)

    copies = []
    for n, (i, j) in enumerate(NEIGHBOURS):
        for k, (src, dst, width) in enumerate(((mb_in, mb_out, 3), (np_in, np_out, 1))):
            sx, dx = cut(i, B, width)
            sy, dy = cut(j, B, width)
            copies.append(
                pltpu.make_async_remote_copy(
                    src_ref=src.at[ds(sx), ds(sy)],
                    dst_ref=dst.at[ds(dx), ds(dy)],
                    send_sem=send.at[n, k],
                    recv_sem=recv.at[n, k],
                    device_id=there(i, j),
                    device_id_type=MESH,
                )
            )
        copies.append(
            pltpu.make_async_remote_copy(
                src_ref=pm_in,
                dst_ref=pm_out.at[pl.ds(2 * (1 - i), 2), 1 - j],
                send_sem=send.at[n, 2],
                recv_sem=recv.at[n, 2],
                device_id=there(i, j),
                device_id_type=MESH,
            )
        )
    for c in copies:
        c.start()
    own = [
        pltpu.make_async_copy(mb_in, mb_out.at[pl.ds(3, B), pl.ds(3, B)], local.at[0]),
        pltpu.make_async_copy(np_in, np_out.at[pl.ds(1, B), pl.ds(1, B)], local.at[1]),
        pltpu.make_async_copy(pm_in, pm_out.at[pl.ds(2, 2), 1], local.at[2]),
    ]
    for c in own:
        c.start()
    for c in own:
        c.wait()
    for c in copies:
        c.wait()


def decode(entries, log_y, first_x, first_y, reach, log_z):
    x = (entries >> (log_y + log_z)) - first_x + reach
    y = ((entries >> log_z) & ((1 << log_y) - 1)) - first_y + reach
    return x * (2 * reach + 1) + y, entries & ((1 << log_z) - 1)


def near_kernel(log_y, list_ref, cs_ref, np_ref, out_ref):
    gx = lax.axis_index("group")
    gy = lax.axis_index("dev")
    row8 = iota((8, WIDTH), 0)
    lane8 = iota((8, WIDTH), 1)
    lane_box = lane8 // PTS
    cols = {}
    for x in range(6):
        for y in range(6):
            tile = np_ref[x, y].astype(F32)
            feat, charge = tile[0:8], tile[8:16]
            lo = jnp.concatenate([feat[3:6], jnp.zeros((5, WIDTH), F32)], axis=0)
            pos = jnp.where(row8 < 3, feat + lo, 0.0)
            sx = B * SCALE * ((x == 5) - (x == 0))
            sy = B * SCALE * ((y == 5) - (y == 0))
            if sx or sy:
                pos = pos + jnp.where(row8 == 0, sx, jnp.where(row8 == 1, sy, 0.0))
            hi, lo = split2(pos)
            tight = hi + lo
            norm = -0.5 * jnp.sum(tight * tight, axis=0, keepdims=True)
            cols[x, y] = (hi, lo, norm, charge.astype(BF))

    def three(v):
        h, l = split2(v)
        return h, l, (v - h - l).astype(BF).astype(F32)

    def spread(v):
        return jnp.broadcast_to(v, (8, WIDTH))

    def twice(v):
        return jnp.where(row8 < 3, v, jnp.concatenate([v[5:8], v[0:5]], axis=0))

    src = {}
    for key, (hi, lo, norm, charge) in cols.items():
        nh, nm, nl = (spread(v) for v in three(norm))
        s0 = jnp.where(row8 < 6, twice(hi), jnp.where(row8 == 6, nh, nm))
        s1 = jnp.where(row8 < 6, twice(lo), jnp.where(row8 == 6, nl, 1.0))
        src[key] = (s0, s1, charge)
    ones2 = jnp.where(row8 < 2, 1.0, 0.0)
    eye = (iota((WIDTH, WIDTH), 0) == iota((WIDTH, WIDTH), 1)).astype(BF)
    outs = []
    for c in range(16):
        x, y = c // B, c % B
        hi, lo, norm, _ = cols[x + 1, y + 1]
        nh, nm, nl = (spread(v) for v in three(norm + LOG_LONG))
        a = jnp.where(row8 < 3, hi, jnp.concatenate([lo[5:8], lo[0:5]], axis=0))
        t0 = jnp.where(row8 < 6, a, 1.0)
        t1 = jnp.where(row8 < 6, a, jnp.where(row8 == 6, 1.0, nh))
        t2 = jnp.where(
            row8 < 4,
            jnp.where(row8 == 0, nm, jnp.where(row8 == 1, nl, 0.0)),
            jnp.where(lane_box == row8 - 4, 1.0, 0.0),
        )
        target = jnp.concatenate([t0, t1, t2, jnp.zeros((8, WIDTH), F32)], axis=0).astype(BF)
        target = dot_nt(eye, target).astype(BF)

        entries = list_ref[x, y]
        slot, zs = decode(entries, log_y, B * gx + x, B * gy + y, 1, 2)
        bit = jnp.where(entries >= 0, jnp.int32(1) << jnp.clip(slot + 9 * (zs & 1), 0, 30), 0)
        w0 = jnp.sum(jnp.where(zs < 2, bit, 0), axis=1, keepdims=True)
        w1 = jnp.sum(jnp.where(zs >= 2, bit, 0), axis=1, keepdims=True)
        w0 = jnp.broadcast_to(jnp.concatenate([w0, w0], axis=0), (8, WIDTH))
        w1 = jnp.broadcast_to(jnp.concatenate([w1, w1], axis=0), (8, WIDTH))
        word = jnp.where(lane_box < 2, w0, w1)
        word = jnp.where(lane_box % 2 == 1, word >> 9, word)
        acc = jnp.zeros((WIDTH, RHS), F32)
        for dx in range(3):
            rhs, charge = [], []
            for dy in range(3):
                k = dx * 3 + dy
                pen = jnp.where((word & (1 << k)) != 0, 0.0, PENALTY)
                s0, s1, q = src[x + dx, y + dy]
                s2 = jnp.where(row8 < 4, ones2, pen)
                rhs.append(jnp.concatenate([s0, s1, s2, jnp.zeros((8, WIDTH), F32)], axis=0).astype(BF))
                charge.append(q)
            u = jnp.dot(target, jnp.concatenate(rhs, axis=1), preferred_element_type=F32)
            v = u * RATIO + (LOG_SHORT - RATIO * LOG_LONG)
            kernel = (jnp.exp2(u) + jnp.exp2(v)).astype(BF)
            acc = acc + dot_nt(kernel, jnp.concatenate(charge, axis=1))
        outs.append(acc)
    turned = jnp.concatenate(outs, axis=1).T
    for c in range(16):
        out_ref[c] = turned[8 * c : 8 * c + 8] + NUGGET * cs_ref[c]


def far_kernel(
    log_y, far_ref, coarse_ref, near_ref, mb_ref, pm_ref, bb_ref, wl_ref, wp_ref, down_ref, out_ref, win, lhs, words
):
    gx = lax.axis_index("group")
    gy = lax.axis_index("dev")
    row8 = iota((8, 128), 0)
    lane4 = iota((4, 128), 1)
    row16 = iota((16, 128), 0)

    def fill(x, carry):
        for y in range(10):
            tile = mb_ref[x, y].astype(F32)
            for half in range(2):
                m = tile[8 * half : 8 * half + 8]
                turned = jnp.concatenate([m[4:8], m[0:4]], axis=0)
                first = jnp.where(row8 < 4, m, turned)
                last = jnp.where(row8 < 4, turned, m)
                win[x, y, 0, :, 128 * half : 128 * half + 128] = jnp.concatenate([first, first], axis=0).astype(BF)
                win[x, y, 1, :, 128 * half : 128 * half + 128] = jnp.concatenate([last, last], axis=0).astype(BF)
        return carry

    lax.fori_loop(0, 10, fill, 0)

    for c in range(16):
        x, y = c // B, c % B
        entries = far_ref[x, y]
        slot, zs = decode(entries, log_y, B * gx + x, B * gy + y, 3, 2)
        late = slot >= 25
        bit = jnp.where(entries >= 0, jnp.int32(1) << jnp.clip(jnp.where(late, slot - 25, slot), 0, 30), 0)
        for h in range(2):
            mine = jnp.where(late == (h == 1), bit, 0)
            w = [jnp.sum(jnp.where(zs == z, mine, 0), axis=1, keepdims=True) for z in range(B)]
            for half in range(2):
                pair = jnp.where(
                    lane4 < 64,
                    jnp.broadcast_to(w[2 * half], (4, 128)),
                    jnp.broadcast_to(w[2 * half + 1], (4, 128)),
                )
                wide = jnp.broadcast_to(pair[0:1], (16, 128))
                for z in range(1, B):
                    wide = jnp.where(row16 >= 4 * z, jnp.broadcast_to(pair[z : z + 1], (16, 128)), wide)
                words[h, c, :, 128 * half : 128 * half + 128] = wide

    for dx in range(7):
        for dy in range(7):
            k = dx * 7 + dy
            h, bit = (0, k) if k < 25 else (1, k - 25)

            def mask_rows(x, carry, dx=dx, dy=dy, k=k, h=h, bit=bit):
                for y in range(B):
                    c = x * B + y
                    keep = jnp.where((words[h, c] & (1 << bit)) != 0, 1.0, 0.0).astype(BF)
                    for s in range(2):
                        r = pl.multiple_of(c * 32 + 16 * s, 16)
                        lhs[pl.ds(r, 16), 256 * k : 256 * k + 256] = keep * win[x + dx, y + dy, s]
                return carry

            lax.fori_loop(0, B, mask_rows, 0, unroll=True)
    local = jnp.dot(lhs[...], wl_ref[...], preferred_element_type=F32)

    row16p = iota((16, 128), 0)
    lane2 = iota((2, 128), 1)
    rows = []
    for px in range(2):
        for py in range(2):
            entries = coarse_ref[px, py]
            slot, zs = decode(entries, log_y - 1, 2 * gx + px, 2 * gy + py, 2, 1)
            bit = jnp.where(entries >= 0, jnp.int32(1) << jnp.clip(slot, 0, 30), 0)
            w = [jnp.sum(jnp.where(zs == z, bit, 0), axis=1, keepdims=True) for z in range(2)]
            pair = jnp.where(
                lane2 < 64, jnp.broadcast_to(w[0], (2, 128)), jnp.broadcast_to(w[1], (2, 128))
            )
            wide = jnp.where(
                row16p < 8, jnp.broadcast_to(pair[0:1], (16, 128)), jnp.broadcast_to(pair[1:2], (16, 128))
            )
            parts = []
            for dx in range(5):
                for dy in range(5):
                    k = dx * 5 + dy
                    tile = pm_ref[px + dx, (py + dy) // 2].astype(F32)
                    r = 8 * ((py + dy) % 2)
                    m = tile[r : r + 8]
                    m = jnp.concatenate([m, m], axis=0)
                    parts.append(jnp.where((wide & (1 << k)) != 0, m, 0.0))
            parts.append(jnp.zeros((16, 128), F32))
            rows.append(jnp.concatenate(parts, axis=1).astype(BF))
    parent = jnp.dot(jnp.concatenate(rows, axis=0), wp_ref[...], preferred_element_type=F32)
    lane8 = iota((8, 128), 1)
    picked = jnp.concatenate(
        [jnp.where(lane8 < 64, parent[16 * q : 16 * q + 8], parent[16 * q + 8 : 16 * q + 16]) for q in range(4)],
        axis=0,
    ).astype(BF)
    descent = jnp.dot(picked, down_ref[...], preferred_element_type=F32)

    lane_z = iota((4, 256), 1) // RANK
    for c in range(16):
        x, y = c // B, c % B
        halves = []
        for s in range(2):
            block = local[c * 32 + 16 * s : c * 32 + 16 * s + 16]
            got = block[0:4]
            for z in range(1, B):
                got = jnp.where(lane_z == z, block[4 * z : 4 * z + 4], got)
            halves.append(got)
        q = (x // 2) * 2 + y // 2
        k = (x % 2) * 2 + y % 2
        total = jnp.concatenate(halves, axis=0) + descent[8 * q : 8 * q + 8, 256 * k : 256 * k + 256]
        far = jnp.dot(total.astype(BF), bb_ref[c], preferred_element_type=F32)
        out_ref[:, x, y, :] = near_ref[c] + far


def vmem(n):
    return [pl.BlockSpec(memory_space=pltpu.VMEM)] * n


def params(mib, **kw):
    return pltpu.CompilerParams(vmem_limit_bytes=mib << 20, **kw)


def on_device(count_g, count_d, wl, wp, up, down, coords, charges, order, near_list, far_list, coarse_list):
    log_y = (count_d * B).bit_length() - 1
    sds = jax.ShapeDtypeStruct
    cs, near_pay, moments, parents, basis = pl.pallas_call(
        prep_kernel,
        out_shape=(
            sds((16, RHS, WIDTH), F32),
            sds((B, B, 16, WIDTH), BF),
            sds((B, B, 16, 128), BF),
            sds((2, 16, 128), BF),
            sds((16, B * RANK, WIDTH), BF),
        ),
        in_specs=vmem(4),
        out_specs=tuple(vmem(5)),
        compiler_params=params(32),
        name="prep",
    )(coords, charges, order, up)
    near_halo, moment_halo, parent_halo = pl.pallas_call(
        functools.partial(exchange_kernel, count_g, count_d),
        out_shape=(
            sds((6, 6, 16, WIDTH), BF),
            sds((10, 10, 16, 128), BF),
            sds((6, 3, 16, 128), BF),
        ),
        in_specs=vmem(3),
        out_specs=tuple(vmem(3)),
        scratch_shapes=[
            pltpu.SemaphoreType.DMA((8, 3)),
            pltpu.SemaphoreType.DMA((8, 3)),
            pltpu.SemaphoreType.DMA((3,)),
        ],
        compiler_params=params(16, collective_id=0, has_side_effects=True),
        name="exchange",
    )(near_pay, moments, parents)
    near = pl.pallas_call(
        functools.partial(near_kernel, log_y),
        out_shape=sds((16, RHS, WIDTH), F32),
        in_specs=vmem(3),
        out_specs=vmem(1)[0],
        compiler_params=params(32),
        name="near",
    )(near_list.transpose(1, 2, 3, 0), cs, near_halo)
    return pl.pallas_call(
        functools.partial(far_kernel, log_y),
        out_shape=sds((RHS, B, B, WIDTH), F32),
        in_specs=vmem(9),
        out_specs=vmem(1)[0],
        scratch_shapes=[
            pltpu.VMEM((10, 10, 2, 16, 256), BF),
            pltpu.VMEM((512, 49 * 256), BF),
            pltpu.VMEM((2, 16, 16, 256), jnp.int32),
        ],
        compiler_params=params(48),
        name="far",
    )(
        far_list.transpose(1, 2, 3, 0),
        coarse_list.transpose(1, 2, 3, 0),
        near,
        moment_halo,
        parent_halo,
        basis,
        wl,
        wp,
        down,
    )


def solution(mesh):
    placed = (
        P(None, "group", "dev", None),
        P(None, "group", "dev", None),
        P("group", "dev", None),
        P(None, "group", "dev", None),
        P(None, "group", "dev", None),
        P(None, "group", "dev", None),
    )
    up, down = transfer_weights()
    wl, wp = leaf_weights(), parent_weights()

    def body(*args):
        return on_device(
            mesh.shape["group"],
            mesh.shape["dev"],
            jnp.asarray(wl),
            jnp.asarray(wp),
            jnp.asarray(up),
            jnp.asarray(down),
            *args,
        )

    return jax.shard_map(
        body,
        mesh=mesh,
        in_specs=placed,
        out_specs=P(None, "group", "dev", None),
        check_vma=False,
    )
```

profile of v0, /device:TPU:1, one launch (start us, length us, event | category | flops | bytes accessed | tf_op | source)
XLA Modules:
  0.0 46.6 jit_solution(11926940687823012842)
XLA Ops:
  0.0 0.0 copy-start.2
  0.0 0.9 %copy-done.2 = bf16[1024,128]{1,0:T(8,128)(2,1)S(1)} copy-done((bf16[1024,128]{1,0:T(8,128)(2,1)S(1)}, bf16[1024,128]{1,0:T(8,128)(2,1)}, u32[]{:S(2)}) %copy-start.2) | copy-done | bytes 262168
  1.0 0.0 copy-start.4
  1.0 0.8 %copy-done.4 = f32[8,4,4,128]{3,2,1,0:T(4,128)S(1)} copy-done((f32[8,4,4,128]{3,2,1,0:T(4,128)S(1)}, f32[8,4,4,128]{3,2,1,0:T(4,128)}, u32[]{:S(2)}) %copy-start.4) | copy-done | bytes 65560
  1.8 0.0 copy-start.6
  1.8 0.7 %copy-done.6 = f32[3,4,4,128]{3,2,1,0:T(4,128)S(1)} copy-done((f32[3,4,4,128]{3,2,1,0:T(4,128)S(1)}, f32[3,4,4,128]{3,2,1,0:T(4,128)}, u32[]{:S(2)}) %copy-start.6) | copy-done | bytes 24600
  2.5 0.0 copy-start.7
  2.5 0.7 %copy-done.7 = s32[4,4,128]{2,1,0:T(4,128)S(1)} copy-done((s32[4,4,128]{2,1,0:T(4,128)S(1)}, s32[4,4,128]{2,1,0:T(4,128)}, u32[]{:S(2)}) %copy-start.7) | copy-done | bytes 8216
  3.2 1.1 %prep.1 = (f32[16,8,128]{2,1,0:T(8,128)S(1)}, bf16[4,4,16,128]{3,2,1,0:T(8,128)(2,1)S(1)}, bf16[4,4,16,128]{3,2,1,0:T(8,128)(2,1)S(1)}, bf16[2,16,128]{2,1,0:T(8,128)(2,1)S(1)}, bf16[16,256,128]{2,1,0:T(8,128)(2,1)S(1)}) custom-call(f32[3,4,4,128]{3,2,1,0:T(4,128)S(1)} %copy-done.6, f32[8,4,4,128]{3,2,1,0:T(4,128)S(1)} %copy-done.4, ...), custom_call_target="tpu_custom_call" | custom-call | tf_op jit(solution)/shard_map/prep/pallas_call | solution.py:464
  4.3 20.7 %exchange.1 = (bf16[6,6,16,128]{3,2,1,0:T(8,128)(2,1)S(1)}, bf16[10,10,16,128]{3,2,1,0:T(8,128)(2,1)S(1)}, bf16[6,3,16,128]{3,2,1,0:T(8,128)(2,1)S(1)}) custom-call(bf16[4,4,16,128]{3,2,1,0:T(8,128)(2,1)S(1)} %get-tuple-element.14.np_in, bf16[4,4,16,128]{3,2,1,0:T(8,128)(2,1)S(1)} %get-tuple-element.15.mb_in, bf16[2,16,128]{2,1,0:T(8,128)(2,1)S(1)} %get-tuple-element.16.pm_in), custom_call_target="tpu_custom_call" | custom-call | tf_op jit(solution)/shard_map/exchange/pallas_call | solution.py:478
  25.0 0.0 copy-start.5
  25.0 0.7 %copy-done.5 = s32[27,4,4,4]{0,3,2,1:T(4,128)S(1)} copy-done((s32[27,4,4,4]{0,3,2,1:T(4,128)S(1)}, s32[27,4,4,4]{0,3,2,1:T(4,128)}, u32[]{:S(2)}) %copy-start.5) | copy-done | bytes 6936
  25.8 9.3 %near.1.near_ref = f32[16,8,128]{2,1,0:T(8,128)S(1)} custom-call(s32[4,4,4,27]{3,2,1,0:T(4,128)S(1)} %bitcast.4, f32[16,8,128]{2,1,0:T(8,128)S(1)} %get-tuple-element.13.cs_ref, bf16[6,6,16,128]{3,2,1,0:T(8,128)(2,1)S(1)} %get-tuple-element.17.np_ref), custom_call_target="tpu_custom_call" | custom-call | tf_op jit(solution)/shard_map/near/pallas_call | solution.py:495
  35.1 0.0 copy-start
  35.1 1.1 %copy-done = bf16[3328,128]{1,0:T(8,128)(2,1)S(1)} copy-done((bf16[3328,128]{1,0:T(8,128)(2,1)S(1)}, bf16[3328,128]{1,0:T(8,128)(2,1)}, u32[]{:S(2)}) %copy-start) | copy-done | bytes 851992
  36.2 0.0 copy-start.1
  36.2 0.9 %copy-done.1 = bf16[128,1024]{1,0:T(8,128)(2,1)S(1)} copy-done((bf16[128,1024]{1,0:T(8,128)(2,1)S(1)}, bf16[128,1024]{1,0:T(8,128)(2,1)}, u32[]{:S(2)}) %copy-start.1) | copy-done | bytes 262168
  37.2 0.0 copy-start.3
  37.2 0.8 %copy-done.3 = s32[138,4,4,4]{0,3,2,1:T(4,128)S(1)} copy-done((s32[138,4,4,4]{0,3,2,1:T(4,128)S(1)}, s32[138,4,4,4]{0,3,2,1:T(4,128)}, u32[]{:S(2)}) %copy-start.3) | copy-done | bytes 35352
  38.0 0.0 copy-start.8
  38.0 0.7 %copy-done.8 = s32[32,2,2,2]{0,3,2,1:T(2,128)S(1)} copy-done((s32[32,2,2,2]{0,3,2,1:T(2,128)S(1)}, s32[32,2,2,2]{0,3,2,1:T(2,128)}, u32[]{:S(2)}) %copy-start.8) | copy-done | bytes 1048
  38.7 7.9 %far.1 = f32[8,4,4,128]{3,2,1,0:T(4,128)} custom-call(s32[4,4,4,138]{3,2,1,0:T(4,128)S(1)} %bitcast.3, s32[2,2,2,32]{3,2,1,0:T(2,128)S(1)} %bitcast.5, f32[16,8,128]{2,1,0:T(8,128)S(1)} %near.1.near_ref, bf16[10,10,16,128]{3,2,1,0:T(8,128)(2,1)S(1)} %get-tuple-element.18.mb_ref, bf16[6,3,16,128]{3,2,1,0:T(8,128)(2,1)S(1)} %get-tuple-element.19.pm_ref, ...), custom_call_target="tpu_custom_call" | custom-call | tf_op jit(solution)/shard_map/far/pallas_call | solution.py:503
Async XLA Ops:
  0.0 0.9 %copy-start.2 = (bf16[1024,128]{1,0:T(8,128)(2,1)S(1)}, bf16[1024,128]{1,0:T(8,128)(2,1)}, u32[]{:S(2)}) copy-start(bf16[1024,128]{1,0:T(8,128)(2,1)} %constant.10.clone.up_ref) | copy-start | bytes 786436
  1.0 0.8 %copy-start.4 = (f32[8,4,4,128]{3,2,1,0:T(4,128)S(1)}, f32[8,4,4,128]{3,2,1,0:T(4,128)}, u32[]{:S(2)}) copy-start(f32[8,4,4,128]{3,2,1,0:T(4,128)} %charges_ref.1) | copy-start | bytes 196612
  1.8 0.7 %copy-start.6 = (f32[3,4,4,128]{3,2,1,0:T(4,128)S(1)}, f32[3,4,4,128]{3,2,1,0:T(4,128)}, u32[]{:S(2)}) copy-start(f32[3,4,4,128]{3,2,1,0:T(4,128)} %coords_ref.1) | copy-start | bytes 73732
  2.5 0.7 %copy-start.7 = (s32[4,4,128]{2,1,0:T(4,128)S(1)}, s32[4,4,128]{2,1,0:T(4,128)}, u32[]{:S(2)}) copy-start(s32[4,4,128]{2,1,0:T(4,128)} %order_ref.1) | copy-start | bytes 24580
  25.0 0.8 %copy-start.5 = (s32[27,4,4,4]{0,3,2,1:T(4,128)S(1)}, s32[27,4,4,4]{0,3,2,1:T(4,128)}, u32[]{:S(2)}) copy-start(s32[27,4,4,4]{0,3,2,1:T(4,128)} %param.13) | copy-start | bytes 20740
  35.1 1.2 %copy-start = (bf16[3328,128]{1,0:T(8,128)(2,1)S(1)}, bf16[3328,128]{1,0:T(8,128)(2,1)}, u32[]{:S(2)}) copy-start(bf16[3328,128]{1,0:T(8,128)(2,1)} %constant.9.clone.wp_ref) | copy-start | bytes 2555908
  36.2 0.9 %copy-start.1 = (bf16[128,1024]{1,0:T(8,128)(2,1)S(1)}, bf16[128,1024]{1,0:T(8,128)(2,1)}, u32[]{:S(2)}) copy-start(bf16[128,1024]{1,0:T(8,128)(2,1)} %constant.11.clone.down_ref) | copy-start | bytes 786436
  37.2 0.8 %copy-start.3 = (s32[138,4,4,4]{0,3,2,1:T(4,128)S(1)}, s32[138,4,4,4]{0,3,2,1:T(4,128)}, u32[]{:S(2)}) copy-start(s32[138,4,4,4]{0,3,2,1:T(4,128)} %param.14) | copy-start | bytes 105988
  38.0 0.7 %copy-start.8 = (s32[32,2,2,2]{0,3,2,1:T(2,128)S(1)}, s32[32,2,2,2]{0,3,2,1:T(2,128)}, u32[]{:S(2)}) copy-start(s32[32,2,2,2]{0,3,2,1:T(2,128)} %param.15) | copy-start | bytes 3076
where the time goes:
time: 47.1 us; the launch traced here: 46.6 us
  Pallas kernels  38.9 us (83%)
  local copies, waits for them, and re-layouts  7.6 us (16%)
    pallas_call x1, Pallas kernels, on_device(): pl.pallas_call(functools.partial(exchange_kernel, count_g, count_d), out_...  20.7 us
    pallas_call x1, Pallas kernels, on_device(): pl.pallas_call(functools.partial(near_kernel, log_y), out_shape=sds((16,...  9.31 us
    pallas_call x1, Pallas kernels, on_device(): pl.pallas_call(functools.partial(far_kernel, log_y), out_shape=sds((RHS,...  7.87 us
    unnamed x18, local copies, waits for them, and re-layouts  7.6 us
    pallas_call x1, Pallas kernels, on_device(): pl.pallas_call(prep_kernel, out_shape=(sds((16, RHS, WIDTH), F32), sds((B...  1.09 us

commit v1 on v0

v1 whole, which is shorter than its diff:
```python
import functools
import math

import jax
import jax.numpy as jnp
import ml_dtypes
import numpy as np
from jax import lax
from jax.experimental import pallas as pl
from jax.experimental.pallas import tpu as pltpu
from jax.sharding import PartitionSpec as P

MESH = pl.DeviceIdType.MESH
BF = jnp.bfloat16
F32 = jnp.float32

ORDER = 4
LENGTH_SCALE = 2.5
AMPLITUDE = 0.025
SHORT_SCALE = 0.5
SHORT_WEIGHT = 0.1
NUGGET = 0.5
LEAF_HALF = 0.75
PARENT_HALF = 1.25

B = 4
PTS = 32
WIDTH = B * PTS
RHS = 8
RANK = ORDER**3

KAPPA = math.log2(math.e) / LENGTH_SCALE**2
SCALE = math.sqrt(2.0 * KAPPA)
RATIO = (LENGTH_SCALE / SHORT_SCALE) ** 2
LOG_LONG = math.log2(AMPLITUDE)
LOG_SHORT = math.log2(SHORT_WEIGHT)
PENALTY = -1024.0

NODES = np.cos((2.0 * np.arange(ORDER) + 1.0) * (math.pi / (2.0 * ORDER)))
NEIGHBOURS = [(i, j) for i in (-1, 0, 1) for j in (-1, 0, 1) if (i, j) != (0, 0)]


def lagrange_np(values):
    out = []
    for a in range(ORDER):
        col = np.ones_like(values)
        for b in range(ORDER):
            if b != a:
                col = col * (values - NODES[b]) / (NODES[a] - NODES[b])
        out.append(col)
    return np.stack(out, axis=-1)


def coupling_np(half, cell, reach):
    offsets = np.arange(-reach, reach + 1) * cell
    gap = half * NODES[None, :, None] - half * NODES[None, None, :] - offsets[:, None, None]
    total = 0.0
    for amp, scale in ((AMPLITUDE, LENGTH_SCALE), (SHORT_WEIGHT, SHORT_SCALE)):
        f = np.exp(-gap * gap / scale**2)
        total = total + amp * np.einsum("xad,ybe,zcf->xyzabcdef", f, f, f)
    n = 2 * reach + 1
    return total.reshape(n, n, n, RANK, RANK)


def leaf_weights():
    table = coupling_np(LEAF_HALF, 1.0, 3)
    w = np.zeros((49, B, RANK, B, RANK))
    for zs in range(B):
        for zt in range(B):
            w[:, zs, :, zt, :] = table[:, :, zs - zt + 3].reshape(49, RANK, RANK).transpose(0, 2, 1)
    return w.reshape(49 * B * RANK, B * RANK).astype(ml_dtypes.bfloat16)


def parent_weights():
    table = coupling_np(PARENT_HALF, 2.0, 2)
    w = np.zeros((26, 2, RANK, 2, RANK))
    for zs in range(2):
        for zt in range(2):
            w[:25, zs, :, zt, :] = table[:, :, zs - zt + 2].reshape(25, RANK, RANK).transpose(0, 2, 1)
    return w.reshape(26 * 2 * RANK, 2 * RANK).astype(ml_dtypes.bfloat16)


def transfer_weights():
    shifts = np.array([-0.5, 0.5])
    f = lagrange_np((shifts[:, None] + LEAF_HALF * NODES[None, :]) / PARENT_HALF)
    t = np.einsum("xad,ybe,zcf->xyzabcdef", f, f, f).reshape(2, 2, 2, RANK, RANK)
    up = np.zeros((2, 2, B, RANK, 2, RANK))
    for z in range(B):
        up[:, :, z, :, z // 2, :] = t[:, :, z % 2]
    up = up.reshape(4, B * RANK, 2 * RANK)
    return (
        up.reshape(4 * B * RANK, 2 * RANK).astype(ml_dtypes.bfloat16),
        up.transpose(2, 0, 1).reshape(2 * RANK, 4 * B * RANK).astype(ml_dtypes.bfloat16),
    )


def iota(shape, dim):
    return lax.broadcasted_iota(jnp.int32, shape, dim)


def dot_nt(a, b):
    return lax.dot_general(a, b, (((1,), (1,)), ((), ())), preferred_element_type=F32)


def split2(v):
    hi = v.astype(BF).astype(F32)
    return hi, (v - hi).astype(BF).astype(F32)


def prepare(gx, gy, coords_ref, charges_ref, order_ref, up_ref, cs_ref, np_ref, mb_ref, pm_ref, bb_ref):
    cen_x = (B * gx + 2).astype(F32)
    cen_y = (B * gy + 2).astype(F32)
    row8 = iota((8, WIDTH), 0)
    lane8 = iota((8, WIDTH), 1)
    lane_box = lane8 // PTS
    centre = jnp.where(row8 == 0, cen_x, jnp.where(row8 == 1, cen_y, 2.0))
    sources = []
    for c in range(16):
        q = charges_ref[:, c // B, c % B, :]
        xyz = coords_ref[:, c // B, c % B, :]
        xyz = jnp.concatenate([xyz, jnp.zeros((5, WIDTH), F32)], axis=0) - jnp.where(
            row8 < 3, centre, 0.0
        )
        sources.append((q, xyz))
    moments = []
    for c in range(16):
        x, y = c // B, c % B
        order = jnp.broadcast_to(order_ref[x, y : y + 1, :], (8, WIDTH))
        hi = order // WIDTH
        lo = order % WIDTH
        q = jnp.zeros((8, WIDTH), F32)
        xyz = jnp.zeros((8, WIDTH), F32)
        for k in range(16):
            here = hi == k
            q = jnp.where(here, jnp.take_along_axis(sources[k][0], lo, axis=1), q)
            xyz = jnp.where(here, jnp.take_along_axis(sources[k][1], lo, axis=1), xyz)
        cs_ref[c] = q
        q_low = q.astype(BF)
        hi2, lo2 = split2(xyz * SCALE)
        lo3 = jnp.concatenate([jnp.zeros((3, WIDTH), F32), lo2[0:5]], axis=0)
        feat = jnp.where(row8 < 3, hi2, lo3)
        np_ref[x, y] = jnp.concatenate([feat, q_low.astype(F32)], axis=0).astype(BF)

        box_centre = jnp.where(
            row8 == 0, x - 1.5, jnp.where(row8 == 1, y - 1.5, lane_box.astype(F32) - 1.5)
        )
        u = (xyz - box_centre) * (1.0 / LEAF_HALF)
        diffs = [u - float(NODES[k]) for k in range(ORDER)]
        polys = []
        for a in range(ORDER):
            denom = 1.0
            poly = None
            for b in range(ORDER):
                if b != a:
                    denom *= float(NODES[a] - NODES[b])
                    poly = diffs[b] if poly is None else poly * diffs[b]
            polys.append(poly * (1.0 / denom))

        def spread(k, d):
            return jnp.broadcast_to(polys[k][d : d + 1, :], (8, WIDTH))

        r4 = row8 % 4
        z8 = jnp.where(
            r4 < 2,
            jnp.where(r4 == 0, spread(0, 2), spread(1, 2)),
            jnp.where(r4 == 2, spread(2, 2), spread(3, 2)),
        )
        yz = [jnp.where(row8 < 4, spread(2 * j, 1), spread(2 * j + 1, 1)) * z8 for j in range(2)]
        basis = jnp.concatenate([spread(a, 0) * yz[j] for a in range(ORDER) for j in range(2)], axis=0)
        lane64 = iota((RANK, WIDTH), 1) // PTS
        wide = jnp.concatenate([jnp.where(lane64 == z, basis, 0.0) for z in range(B)], axis=0).astype(BF)
        bb_ref[c] = wide
        m = dot_nt(q_low, wide).astype(BF)
        moments.append(m)
        m32 = m.astype(F32)
        mb_ref[x, y] = jnp.concatenate([m32[:, :128], m32[:, 128:]], axis=0).astype(BF)
    for px in range(2):
        rows = []
        for py in range(2):
            kids = [moments[(2 * px + sx) * B + 2 * py + sy].astype(F32) for sx in range(2) for sy in range(2)]
            rows.append(jnp.concatenate(kids, axis=1))
        lhs = jnp.concatenate(rows, axis=0).astype(BF)
        pm_ref[px] = jnp.dot(lhs, up_ref[...], preferred_element_type=F32).astype(BF)


def cut(side, size, width):
    if side == 0:
        return pl.ds(0, size), pl.ds(width, size)
    if side > 0:
        return pl.ds(size - width, width), pl.ds(0, width)
    return pl.ds(0, width), pl.ds(width + size, width)


def decode(entries, log_y, first_x, first_y, reach, log_z):
    x = (entries >> (log_y + log_z)) - first_x + reach
    y = ((entries >> log_z) & ((1 << log_y) - 1)) - first_y + reach
    return x, y, entries & ((1 << log_z) - 1)


def one_bit(entries, position):
    return jnp.where(entries >= 0, jnp.int32(1) << jnp.clip(position, 0, 30), 0)


def main_kernel(
    count_g,
    count_d,
    log_y,
    coords_in,
    charges_in,
    order_in,
    near_in,
    far_in,
    coarse_in,
    up_in,
    wl_in,
    wp_in,
    down_in,
    out_ref,
    coords,
    charges,
    order,
    near_list,
    far_list,
    coarse_list,
    up,
    wl,
    wp,
    down,
    cs,
    np_in,
    mb_in,
    pm_in,
    basis,
    near_out,
    np_halo,
    mb_halo,
    pm_halo,
    win,
    lhs,
    words,
    targets,
    near_words,
    load_sem,
    send,
    recv,
):
    g = lax.axis_index("group")
    d = lax.axis_index("dev")

    def there(i, j):
        return (lax.rem(g + i + count_g, count_g), lax.rem(d + j + count_d, count_d))

    loads = [
        pltpu.make_async_copy(src, dst, load_sem.at[n])
        for n, (src, dst) in enumerate(
            (
                (coords_in, coords),
                (charges_in, charges),
                (order_in, order),
                (up_in, up),
                (near_in, near_list),
                (far_in, far_list),
                (coarse_in, coarse_list),
                (wp_in, wp),
                (down_in, down),
                (wl_in, wl),
            )
        )
    ]
    for load in loads:
        load.start()

    barrier = pltpu.get_barrier_semaphore()
    for i, j in NEIGHBOURS:
        pl.semaphore_signal(barrier, inc=1, device_id=there(i, j), device_id_type=MESH)
    for load in loads[:4]:
        load.wait()
    prepare(g, d, coords, charges, order, up, cs, np_in, mb_in, pm_in, basis)
    pl.semaphore_wait(barrier, len(NEIGHBOURS))

    def remote(n, k, src, dst):
        return pltpu.make_async_remote_copy(
            src_ref=src,
            dst_ref=dst,
            send_sem=send.at[n, k],
            recv_sem=recv.at[n, k],
            device_id=there(*NEIGHBOURS[n]),
            device_id_type=MESH,
        )

    near_copies, moment_copies, parent_copies = [], [], []
    for n, (i, j) in enumerate(NEIGHBOURS):
        (sx, tx), (sy, ty) = cut(i, B, 1), cut(j, B, 1)
        near_copies.append(remote(n, 0, np_in.at[sx, sy], np_halo.at[tx, ty]))
        (sx, tx), (sy, ty) = cut(i, B, 3), cut(j, B, 3)
        moment_copies.append(remote(n, 1, mb_in.at[sx, sy], mb_halo.at[tx, ty]))
        parent_copies.append(remote(n, 2, pm_in, pm_halo.at[pl.ds(2 * (1 - i), 2), 1 - j]))
    for copy in near_copies + moment_copies + parent_copies:
        copy.start()

    row8 = iota((8, WIDTH), 0)
    lane8 = iota((8, WIDTH), 1)
    lane_box = lane8 // PTS
    lane4 = iota((4, 128), 1)
    row16 = iota((16, 128), 0)
    zeros8 = jnp.zeros((8, WIDTH), F32)

    def column(tile, sx, sy):
        feat, charge = tile[0:8], tile[8:16]
        lo = jnp.concatenate([feat[3:6], jnp.zeros((5, WIDTH), F32)], axis=0)
        pos = jnp.where(row8 < 3, feat + lo, 0.0)
        if sx or sy:
            pos = pos + jnp.where(row8 == 0, B * SCALE * sx, jnp.where(row8 == 1, B * SCALE * sy, 0.0))
        hi, lo = split2(pos)
        tight = hi + lo
        norm = -0.5 * jnp.sum(tight * tight, axis=0, keepdims=True)
        return hi, lo, norm, charge.astype(BF)

    def three(v):
        h, m = split2(v)
        low = (v - h - m).astype(BF).astype(F32)
        return [jnp.broadcast_to(part, (8, WIDTH)) for part in (h, m, low)]

    def twice(v):
        return jnp.where(row8 < 3, v, jnp.concatenate([v[5:8], v[0:5]], axis=0))

    def source(col):
        hi, lo, norm, charge = col
        nh, nm, nl = three(norm)
        s0 = jnp.where(row8 < 6, twice(hi), jnp.where(row8 == 6, nh, nm))
        s1 = jnp.where(row8 < 6, twice(lo), jnp.where(row8 == 6, nl, 1.0))
        return s0, s1, charge

    ones2 = jnp.where(row8 < 2, 1.0, 0.0)

    def pairs(target, word, sources):
        rhs = []
        for slot, (s0, s1, _) in sources:
            pen = jnp.where((word & (1 << slot)) != 0, 0.0, PENALTY)
            rhs.append(jnp.concatenate([s0, s1, jnp.where(row8 < 4, ones2, pen), zeros8], axis=0).astype(BF))
        u = jnp.dot(target, jnp.concatenate(rhs, axis=1), preferred_element_type=F32)
        kernel = jnp.exp2(u) + jnp.exp2(u * RATIO + (LOG_SHORT - RATIO * LOG_LONG))
        return dot_nt(kernel.astype(BF), jnp.concatenate([s[2] for _, s in sources], axis=1))

    def window(x, y, tile):
        for half in range(2):
            m = tile[8 * half : 8 * half + 8].astype(F32)
            turned = jnp.concatenate([m[4:8], m[0:4]], axis=0)
            first = jnp.where(row8 < 4, m, turned)
            last = jnp.where(row8 < 4, turned, m)
            lanes = slice(128 * half, 128 * half + 128)
            win[x, y, 0, :, lanes] = jnp.concatenate([first, first], axis=0).astype(BF)
            win[x, y, 1, :, lanes] = jnp.concatenate([last, last], axis=0).astype(BF)

    def lhs_at(x, dx, y, dy, s):
        rows = pl.ds(pl.multiple_of(x * 128 + y * 32 + 16 * s, 16), 16)
        return rows, pl.ds(pl.multiple_of(dx * 1792 + 256 * dy, 256), 256)

    def multiply(x, dx, y, dy):
        for s in range(2):
            rows, lanes = lhs_at(x, dx, y, dy, s)
            lhs[rows, lanes] = lhs[rows, lanes] * win[x + dx, y + dy, s]

    def halo_shift(x, t):
        return t + 4 * ((x + t) // 3)

    for load in loads[4:9]:
        load.wait()

    def far_words(x, carry):
        for y in range(B):
            entries = far_list[x, y]
            ox, oy, zs = decode(entries, log_y, B * g + x, B * d + y, 3, 2)
            late = oy >= 4
            bit = one_bit(entries, jnp.where(late, 3 * ox + oy - 4, 4 * ox + oy))
            for h in range(2):
                mine = jnp.where(late == (h == 1), bit, 0)
                w = [jnp.sum(jnp.where(zs == z, mine, 0), axis=1, keepdims=True) for z in range(B)]
                for half in range(2):
                    pair = jnp.where(
                        lane4 < 64,
                        jnp.broadcast_to(w[2 * half], (4, 128)),
                        jnp.broadcast_to(w[2 * half + 1], (4, 128)),
                    )
                    wide = jnp.broadcast_to(pair[0:1], (16, 128))
                    for z in range(1, B):
                        wide = jnp.where(row16 >= 4 * z, jnp.broadcast_to(pair[z : z + 1], (16, 128)), wide)
                    words[h, x, y, :, 128 * half : 128 * half + 128] = wide
        return carry

    lax.fori_loop(0, B, far_words, 0)

    def masks(n, carry):
        x, dx = n // 7, n % 7
        for y in range(B):
            w0 = words[0, x, y] >> (4 * dx)
            w1 = words[1, x, y] >> (3 * dx)
            for dy in range(7):
                w, bit = (w0, dy) if dy < 4 else (w1, dy - 4)
                keep = jnp.where((w & (1 << bit)) != 0, 1.0, 0.0).astype(BF)
                for s in range(2):
                    rows, lanes = lhs_at(x, dx, y, dy, s)
                    lhs[rows, lanes] = keep
        return carry

    lax.fori_loop(0, 28, masks, 0)

    def own_windows(x, carry):
        for y in range(B):
            window(x + 3, y + 3, mb_in[x, y])
        return carry

    lax.fori_loop(0, B, own_windows, 0)

    def own_products(n, carry):
        x = n // 4
        dx = 3 - x + n % 4
        for y in range(B):
            for dy in range(3 - y, 7 - y):
                multiply(x, dx, y, dy)
        return carry

    lax.fori_loop(0, 16, own_products, 0)

    own = {}
    for x in range(B):
        for y in range(B):
            own[x, y] = column(np_in[x, y].astype(F32), 0, 0)
    own_source = {key: source(col) for key, col in own.items()}
    eye = (iota((WIDTH, WIDTH), 0) == iota((WIDTH, WIDTH), 1)).astype(BF)
    outs = []
    for c in range(16):
        x, y = c // B, c % B
        hi, lo, norm, _ = own[x, y]
        nh, nm, nl = three(norm + LOG_LONG)
        a = jnp.where(row8 < 3, hi, jnp.concatenate([lo[5:8], lo[0:5]], axis=0))
        t0 = jnp.where(row8 < 6, a, 1.0)
        t1 = jnp.where(row8 < 6, a, jnp.where(row8 == 6, 1.0, nh))
        t2 = jnp.where(
            row8 < 4,
            jnp.where(row8 == 0, nm, jnp.where(row8 == 1, nl, 0.0)),
            jnp.where(lane_box == row8 - 4, 1.0, 0.0),
        )
        target = dot_nt(eye, jnp.concatenate([t0, t1, t2, zeros8], axis=0).astype(BF)).astype(BF)
        targets[c] = target

        entries = near_list[x, y]
        ox, oy, zs = decode(entries, log_y, B * g + x, B * d + y, 1, 2)
        bit = one_bit(entries, 3 * ox + oy + 9 * (zs & 1))
        w0 = jnp.sum(jnp.where(zs < 2, bit, 0), axis=1, keepdims=True)
        w1 = jnp.sum(jnp.where(zs >= 2, bit, 0), axis=1, keepdims=True)
        w0 = jnp.broadcast_to(jnp.concatenate([w0, w0], axis=0), (8, WIDTH))
        w1 = jnp.broadcast_to(jnp.concatenate([w1, w1], axis=0), (8, WIDTH))
        word = jnp.where(lane_box < 2, w0, w1)
        word = jnp.where(lane_box % 2 == 1, word >> 9, word)
        near_words[c] = word
        acc = jnp.zeros((WIDTH, RHS), F32)
        for dx in (-1, 0, 1):
            sources = [
                (3 * (dx + 1) + dy + 1, own_source[x + dx, y + dy])
                for dy in (-1, 0, 1)
                if (x + dx, y + dy) in own_source
            ]
            if sources:
                acc = acc + pairs(target, word, sources)
        outs.append(acc)
    turned = jnp.concatenate(outs, axis=1).T
    for c in range(16):
        near_out[c] = turned[8 * c : 8 * c + 8]

    pm_halo[pl.ds(2, 2), 1] = pm_in[...]

    for copy in near_copies:
        copy.wait_recv()
    halo_source = {}
    for x in range(6):
        for y in range(6):
            sx, sy = (x == 5) - (x == 0), (y == 5) - (y == 0)
            if sx or sy:
                halo_source[x, y] = source(column(np_halo[x, y].astype(F32), sx, sy))
    outs = []
    for c in range(16):
        x, y = c // B, c % B
        sources = [
            (3 * dx + dy, halo_source[x + dx, y + dy])
            for dx in range(3)
            for dy in range(3)
            if (x + dx, y + dy) in halo_source
        ]
        if sources:
            outs.append(pairs(targets[c], near_words[c], sources))
        else:
            outs.append(jnp.zeros((WIDTH, RHS), F32))
    turned = jnp.concatenate(outs, axis=1).T
    for c in range(16):
        near_out[c] = near_out[c] + turned[8 * c : 8 * c + 8]

    for copy in parent_copies:
        copy.wait_recv()
    lane2 = iota((2, 128), 1)
    rows = []
    for px in range(2):
        for py in range(2):
            entries = coarse_list[px, py]
            ox, oy, zs = decode(entries, log_y - 1, 2 * g + px, 2 * d + py, 2, 1)
            bit = one_bit(entries, 5 * ox + oy)
            w = [jnp.sum(jnp.where(zs == z, bit, 0), axis=1, keepdims=True) for z in range(2)]
            pair = jnp.where(lane2 < 64, jnp.broadcast_to(w[0], (2, 128)), jnp.broadcast_to(w[1], (2, 128)))
            wide = jnp.where(
                row16 < 8, jnp.broadcast_to(pair[0:1], (16, 128)), jnp.broadcast_to(pair[1:2], (16, 128))
            )
            parts = []
            for dx in range(5):
                for dy in range(5):
                    tile = pm_halo[px + dx, (py + dy) // 2].astype(F32)
                    r = 8 * ((py + dy) % 2)
                    m = tile[r : r + 8]
                    m = jnp.concatenate([m, m], axis=0)
                    parts.append(jnp.where((wide & (1 << (5 * dx + dy))) != 0, m, 0.0))
            parts.append(jnp.zeros((16, 128), F32))
            rows.append(jnp.concatenate(parts, axis=1).astype(BF))
    parent = jnp.dot(jnp.concatenate(rows, axis=0), wp[...], preferred_element_type=F32)
    picked = jnp.concatenate(
        [jnp.where(lane8 < 64, parent[16 * q : 16 * q + 8], parent[16 * q + 8 : 16 * q + 16]) for q in range(4)],
        axis=0,
    ).astype(BF)
    descent = jnp.dot(picked, down[...], preferred_element_type=F32)

    for copy in moment_copies:
        copy.wait_recv()
    loads[9].wait()

    def outer_windows(n, carry):
        x = n + 4 * (n // 3)
        for y in range(10):
            window(x, y, mb_halo[x, y])
        return carry

    lax.fori_loop(0, 6, outer_windows, 0)

    def side_windows(x, carry):
        for y in (0, 1, 2, 7, 8, 9):
            window(x, y, mb_halo[x, y])
        return carry

    lax.fori_loop(3, 7, side_windows, 0)

    def outer_products(n, carry):
        x = n // 3
        dx = halo_shift(x, n % 3)
        for y in range(B):
            for dy in range(7):
                multiply(x, dx, y, dy)
        return carry

    lax.fori_loop(0, 12, outer_products, 0)

    def side_products(n, carry):
        x = n // 4
        dx = 3 - x + n % 4
        for y in range(B):
            for t in range(3):
                multiply(x, dx, y, halo_shift(y, t))
        return carry

    lax.fori_loop(0, 16, side_products, 0)
    local = jnp.dot(lhs[...], wl[...], preferred_element_type=F32)

    lane_z = iota((4, 256), 1) // RANK
    for c in range(16):
        x, y = c // B, c % B
        halves = []
        for s in range(2):
            block = local[c * 32 + 16 * s : c * 32 + 16 * s + 16]
            got = block[0:4]
            for z in range(1, B):
                got = jnp.where(lane_z == z, block[4 * z : 4 * z + 4], got)
            halves.append(got)
        q = (x // 2) * 2 + y // 2
        k = (x % 2) * 2 + y % 2
        total = jnp.concatenate(halves, axis=0) + descent[8 * q : 8 * q + 8, 256 * k : 256 * k + 256]
        far = jnp.dot(total.astype(BF), basis[c], preferred_element_type=F32)
        out_ref[:, x, y, :] = NUGGET * cs[c] + near_out[c] + far
    for copy in near_copies + moment_copies + parent_copies:
        copy.wait_send()


def vmem(n):
    return [pl.BlockSpec(memory_space=pltpu.VMEM)] * n


def anywhere(n):
    return [pl.BlockSpec(memory_space=pltpu.HBM)] * n


def params(mib, **kw):
    return pltpu.CompilerParams(vmem_limit_bytes=mib << 20, **kw)


def on_device(count_g, count_d, wl, wp, up, down, coords, charges, order, near_list, far_list, coarse_list):
    log_y = (count_d * B).bit_length() - 1
    near_list = near_list.transpose(1, 2, 3, 0)
    far_list = far_list.transpose(1, 2, 3, 0)
    coarse_list = coarse_list.transpose(1, 2, 3, 0)
    operands = (coords, charges, order, near_list, far_list, coarse_list, up, wl, wp, down)
    return pl.pallas_call(
        functools.partial(main_kernel, count_g, count_d, log_y),
        out_shape=jax.ShapeDtypeStruct((RHS, B, B, WIDTH), F32),
        in_specs=[pl.BlockSpec(memory_space=pl.ANY)] * len(operands),
        out_specs=pl.BlockSpec(memory_space=pltpu.VMEM),
        scratch_shapes=[pltpu.VMEM(a.shape, a.dtype) for a in operands]
        + [
            pltpu.VMEM((16, RHS, WIDTH), F32),
            pltpu.VMEM((B, B, 16, WIDTH), BF),
            pltpu.VMEM((B, B, 16, 128), BF),
            pltpu.VMEM((2, 16, 128), BF),
            pltpu.VMEM((16, B * RANK, WIDTH), BF),
            pltpu.VMEM((16, RHS, WIDTH), F32),
            pltpu.VMEM((6, 6, 16, WIDTH), BF),
            pltpu.VMEM((10, 10, 16, 128), BF),
            pltpu.VMEM((6, 3, 16, 128), BF),
            pltpu.VMEM((10, 10, 2, 16, 256), BF),
            pltpu.VMEM((512, 49 * 256), BF),
            pltpu.VMEM((2, B, B, 16, 256), jnp.int32),
            pltpu.VMEM((16, WIDTH, 32), BF),
            pltpu.VMEM((16, 8, WIDTH), jnp.int32),
            pltpu.SemaphoreType.DMA((len(operands),)),
            pltpu.SemaphoreType.DMA((8, 3)),
            pltpu.SemaphoreType.DMA((8, 3)),
        ],
        compiler_params=pltpu.CompilerParams(
            vmem_limit_bytes=60 << 20, collective_id=0, has_side_effects=True
        ),
        name="fields",
    )(*operands)


def solution(mesh):
    placed = (
        P(None, "group", "dev", None),
        P(None, "group", "dev", None),
        P("group", "dev", None),
        P(None, "group", "dev", None),
        P(None, "group", "dev", None),
        P(None, "group", "dev", None),
    )
    up, down = transfer_weights()
    wl, wp = leaf_weights(), parent_weights()

    def body(*args):
        return on_device(
            mesh.shape["group"],
            mesh.shape["dev"],
            jnp.asarray(wl),
            jnp.asarray(wp),
            jnp.asarray(up),
            jnp.asarray(down),
            *args,
        )

    return jax.shard_map(
        body,
        mesh=mesh,
        in_specs=placed,
        out_specs=P(None, "group", "dev", None),
        check_vma=False,
    )
```

time: 47.1 us -> 37.2 us (0.79)
  the two profiles are of different devices: /device:TPU:1 before, /device:TPU:24 now
where the time goes in v1:
time: 37.2 us; the launch traced here: 37.1 us
  Pallas kernels  35.6 us (96%)
  local copies, waits for them, and re-layouts  1.47 us (4%)
    pallas_call x1, Pallas kernels, on_device(): pl.pallas_call(functools.partial(main_kernel, count_g, count_d, log_y), o...  35.6 us
    unnamed x1, local copies, waits for them, and re-layouts  1.47 us

profile of v1, /device:TPU:24, one launch (start us, length us, event | category | flops | bytes accessed | tf_op | source)
XLA Modules:
  0.0 37.1 jit_solution(14674384073616537623)
XLA Ops:
  0.0 35.6 %fields.1 = f32[8,4,4,128]{3,2,1,0:T(4,128)} custom-call(f32[3,4,4,128]{3,2,1,0:T(4,128)} %coords_in.1, f32[8,4,4,128]{3,2,1,0:T(4,128)} %charges_in.1, s32[4,4,128]{2,1,0:T(4,128)} %order_in.1, s32[4,4,4,27]{3,2,1,0:T(4,128)} %bitcast.4, s32[4,4,4,138]{3,2,1,0:T(4,128)} %bitcast.3, s32[2,2,2,32]{3,2,1,0:T(2,128)} %bitcast.5, ...), custom_call_target="tpu_custom_call" | custom-call | tf_op jit(solution)/shard_map/fields/pallas_call | solution.py:606
  35.6 1.5 %copy.12 = f32[8,4,4,128]{3,2,1,0:T(4,128)} copy(f32[8,4,4,128]{3,2,1,0:T(4,128)} %fields.1) | data formatting | bytes 131072

commit v2 on v1

--- a/solution.py
+++ b/solution.py
@@ -33,7 +33,7 @@
 SCALE = math.sqrt(2.0 * KAPPA)
 RATIO = (LENGTH_SCALE / SHORT_SCALE) ** 2
 LOG_LONG = math.log2(AMPLITUDE)
-LOG_SHORT = math.log2(SHORT_WEIGHT)
+LOG_SHORT = math.log2(SHORT_WEIGHT) - RATIO * LOG_LONG
 PENALTY = -1024.0
 
 NODES = np.cos((2.0 * np.arange(ORDER) + 1.0) * (math.pi / (2.0 * ORDER)))
@@ -239,7 +239,6 @@
     lhs,
     words,
     targets,
-    near_words,
     load_sem,
     send,
     recv,
@@ -324,23 +323,56 @@
     def twice(v):
         return jnp.where(row8 < 3, v, jnp.concatenate([v[5:8], v[0:5]], axis=0))
 
+    own_box = jnp.where(lane_box == row8 - 4, 1.0, 0.0)
+
     def source(col):
         hi, lo, norm, charge = col
         nh, nm, nl = three(norm)
         s0 = jnp.where(row8 < 6, twice(hi), jnp.where(row8 == 6, nh, nm))
         s1 = jnp.where(row8 < 6, twice(lo), jnp.where(row8 == 6, nl, 1.0))
-        return s0, s1, charge
-
-    ones2 = jnp.where(row8 < 2, 1.0, 0.0)
-
-    def pairs(target, word, sources):
-        rhs = []
-        for slot, (s0, s1, _) in sources:
-            pen = jnp.where((word & (1 << slot)) != 0, 0.0, PENALTY)
-            rhs.append(jnp.concatenate([s0, s1, jnp.where(row8 < 4, ones2, pen), zeros8], axis=0).astype(BF))
-        u = jnp.dot(target, jnp.concatenate(rhs, axis=1), preferred_element_type=F32)
-        kernel = jnp.exp2(u) + jnp.exp2(u * RATIO + (LOG_SHORT - RATIO * LOG_LONG))
-        return dot_nt(kernel.astype(BF), jnp.concatenate([s[2] for _, s in sources], axis=1))
+        s2 = jnp.where(row8 < 2, 1.0, own_box)
+        return jnp.concatenate([s0, s1, s2, zeros8], axis=0).astype(BF), charge
+
+    def near_sums(sources, depth=1, width=4):
+        groups = []
+        for (x, y), features in sources.items():
+            near = [
+                (tx * B + ty, 3 * (x - tx) + y - ty)
+                for tx in range(B)
+                for ty in range(B)
+                if 0 <= x - tx < 3 and 0 <= y - ty < 3
+            ]
+            groups += [(features, near[n : n + width]) for n in range(0, len(near), width)]
+        acc = {}
+        exponents, kernels = [], []
+
+        def exponent(n):
+            (feat, _), group = groups[n]
+            return lax.dot_general(
+                feat,
+                jnp.concatenate([targets[c, slot] for c, slot in group], axis=1),
+                (((0,), (0,)), ((), ())),
+                preferred_element_type=F32,
+            )
+
+        def finish(n, kernel):
+            (_, charge), group = groups[n]
+            out = jnp.dot(charge, kernel, preferred_element_type=F32)
+            for i, (c, _) in enumerate(group):
+                part = out[:, 128 * i : 128 * i + 128]
+                acc[c] = part if c not in acc else acc[c] + part
+
+        waiting = []
+        u = exponent(0)
+        for n in range(len(groups)):
+            after = exponent(n + 1) if n + 1 < len(groups) else None
+            waiting.append((n, (jnp.exp2(u) + jnp.exp2(u * RATIO + LOG_SHORT)).astype(BF)))
+            u = after
+            if len(waiting) > depth:
+                finish(*waiting.pop(0))
+        for item in waiting:
+            finish(*item)
+        return acc
 
     def window(x, y, tile):
         for half in range(2):
@@ -353,16 +385,16 @@
             win[x, y, 1, :, lanes] = jnp.concatenate([last, last], axis=0).astype(BF)
 
     def lhs_at(x, dx, y, dy, s):
-        rows = pl.ds(pl.multiple_of(x * 128 + y * 32 + 16 * s, 16), 16)
-        return rows, pl.ds(pl.multiple_of(dx * 1792 + 256 * dy, 256), 256)
-
-    def multiply(x, dx, y, dy):
+        row = x * 128 + y * 32 + 16 * s
+        lane = dx * 1792 + 256 * dy
+        return slice(row, row + 16), slice(lane, lane + 256)
+
+    def is_own(x, dx, y, dy):
+        return 3 <= x + dx < 7 and 3 <= y + dy < 7
+
+    def products(keep, x, dx, y, dy):
         for s in range(2):
-            rows, lanes = lhs_at(x, dx, y, dy, s)
-            lhs[rows, lanes] = lhs[rows, lanes] * win[x + dx, y + dy, s]
-
-    def halo_shift(x, t):
-        return t + 4 * ((x + t) // 3)
+            lhs[lhs_at(x, dx, y, dy, s)] = keep * win[x + dx, y + dy, s]
 
     for load in loads[4:9]:
         load.wait()
@@ -371,8 +403,9 @@
         for y in range(B):
             entries = far_list[x, y]
             ox, oy, zs = decode(entries, log_y, B * g + x, B * d + y, 3, 2)
-            late = oy >= 4
-            bit = one_bit(entries, jnp.where(late, 3 * ox + oy - 4, 4 * ox + oy))
+            slot = 7 * ox + oy
+            late = slot >= 25
+            bit = one_bit(entries, jnp.where(late, slot - 25, slot))
             for h in range(2):
                 mine = jnp.where(late == (h == 1), bit, 0)
                 w = [jnp.sum(jnp.where(zs == z, mine, 0), axis=1, keepdims=True) for z in range(B)]
@@ -390,21 +423,6 @@
 
     lax.fori_loop(0, B, far_words, 0)
 
-    def masks(n, carry):
-        x, dx = n // 7, n % 7
-        for y in range(B):
-            w0 = words[0, x, y] >> (4 * dx)
-            w1 = words[1, x, y] >> (3 * dx)
-            for dy in range(7):
-                w, bit = (w0, dy) if dy < 4 else (w1, dy - 4)
-                keep = jnp.where((w & (1 << bit)) != 0, 1.0, 0.0).astype(BF)
-                for s in range(2):
-                    rows, lanes = lhs_at(x, dx, y, dy, s)
-                    lhs[rows, lanes] = keep
-        return carry
-
-    lax.fori_loop(0, 28, masks, 0)
-
     def own_windows(x, carry):
         for y in range(B):
             window(x + 3, y + 3, mb_in[x, y])
@@ -412,61 +430,46 @@
 
     lax.fori_loop(0, B, own_windows, 0)
 
-    def own_products(n, carry):
-        x = n // 4
-        dx = 3 - x + n % 4
-        for y in range(B):
-            for dy in range(3 - y, 7 - y):
-                multiply(x, dx, y, dy)
-        return carry
-
-    lax.fori_loop(0, 16, own_products, 0)
-
-    own = {}
     for x in range(B):
         for y in range(B):
-            own[x, y] = column(np_in[x, y].astype(F32), 0, 0)
-    own_source = {key: source(col) for key, col in own.items()}
-    eye = (iota((WIDTH, WIDTH), 0) == iota((WIDTH, WIDTH), 1)).astype(BF)
-    outs = []
+            for h, first, last in ((0, 0, 25), (1, 25, 49)):
+                w = words[h, x, y]
+                for slot in range(first, last):
+                    dx, dy = slot // 7, slot % 7
+                    keep = jnp.where((w & (1 << (slot - first))) != 0, 1.0, 0.0).astype(BF)
+                    if is_own(x, dx, y, dy):
+                        products(keep, x, dx, y, dy)
+                    else:
+                        lhs[lhs_at(x, dx, y, dy, 0)] = keep
+
+    own_source = {}
     for c in range(16):
         x, y = c // B, c % B
-        hi, lo, norm, _ = own[x, y]
+        col = column(np_in[x, y].astype(F32), 0, 0)
+        own_source[x + 1, y + 1] = source(col)
+        hi, lo, norm, _ = col
         nh, nm, nl = three(norm + LOG_LONG)
         a = jnp.where(row8 < 3, hi, jnp.concatenate([lo[5:8], lo[0:5]], axis=0))
         t0 = jnp.where(row8 < 6, a, 1.0)
         t1 = jnp.where(row8 < 6, a, jnp.where(row8 == 6, 1.0, nh))
-        t2 = jnp.where(
-            row8 < 4,
-            jnp.where(row8 == 0, nm, jnp.where(row8 == 1, nl, 0.0)),
-            jnp.where(lane_box == row8 - 4, 1.0, 0.0),
-        )
-        target = dot_nt(eye, jnp.concatenate([t0, t1, t2, zeros8], axis=0).astype(BF)).astype(BF)
-        targets[c] = target
+        t2 = jnp.where(row8 == 0, nm, jnp.where(row8 == 1, nl, 0.0))
 
         entries = near_list[x, y]
         ox, oy, zs = decode(entries, log_y, B * g + x, B * d + y, 1, 2)
         bit = one_bit(entries, 3 * ox + oy + 9 * (zs & 1))
-        w0 = jnp.sum(jnp.where(zs < 2, bit, 0), axis=1, keepdims=True)
-        w1 = jnp.sum(jnp.where(zs >= 2, bit, 0), axis=1, keepdims=True)
-        w0 = jnp.broadcast_to(jnp.concatenate([w0, w0], axis=0), (8, WIDTH))
-        w1 = jnp.broadcast_to(jnp.concatenate([w1, w1], axis=0), (8, WIDTH))
-        word = jnp.where(lane_box < 2, w0, w1)
-        word = jnp.where(lane_box % 2 == 1, word >> 9, word)
-        near_words[c] = word
-        acc = jnp.zeros((WIDTH, RHS), F32)
-        for dx in (-1, 0, 1):
-            sources = [
-                (3 * (dx + 1) + dy + 1, own_source[x + dx, y + dy])
-                for dy in (-1, 0, 1)
-                if (x + dx, y + dy) in own_source
-            ]
-            if sources:
-                acc = acc + pairs(target, word, sources)
-        outs.append(acc)
-    turned = jnp.concatenate(outs, axis=1).T
-    for c in range(16):
-        near_out[c] = turned[8 * c : 8 * c + 8]
+        lanes = []
+        for h in range(2):
+            w = jnp.sum(jnp.where((zs >> 1) == h, bit, 0), axis=1, keepdims=True)
+            w = jnp.where(lane4 // PTS == iota((4, 128), 0), jnp.broadcast_to(w, (4, 128)), 0)
+            lanes.append(jnp.broadcast_to(jnp.sum(w, axis=0, keepdims=True), (8, WIDTH)))
+        word = jnp.where(row8 < 6, lanes[0], lanes[1])
+        word = jnp.where(row8 % 2 == 1, word >> 9, word)
+        for slot in range(9):
+            pen = jnp.where((word & (1 << slot)) != 0, 0.0, PENALTY)
+            t = [t0, t1, jnp.where(row8 < 4, t2, pen), zeros8]
+            targets[c, slot] = jnp.concatenate(t, axis=0).astype(BF)
+    for c, part in near_sums(own_source).items():
+        near_out[c] = part
 
     pm_halo[pl.ds(2, 2), 1] = pm_in[...]
 
@@ -478,22 +481,8 @@
             sx, sy = (x == 5) - (x == 0), (y == 5) - (y == 0)
             if sx or sy:
                 halo_source[x, y] = source(column(np_halo[x, y].astype(F32), sx, sy))
-    outs = []
-    for c in range(16):
-        x, y = c // B, c % B
-        sources = [
-            (3 * dx + dy, halo_source[x + dx, y + dy])
-            for dx in range(3)
-            for dy in range(3)
-            if (x + dx, y + dy) in halo_source
-        ]
-        if sources:
-            outs.append(pairs(targets[c], near_words[c], sources))
-        else:
-            outs.append(jnp.zeros((WIDTH, RHS), F32))
-    turned = jnp.concatenate(outs, axis=1).T
-    for c in range(16):
-        near_out[c] = near_out[c] + turned[8 * c : 8 * c + 8]
+    for c, part in near_sums(halo_source).items():
+        near_out[c] = near_out[c] + part
 
     for copy in parent_copies:
         copy.wait_recv()
@@ -545,25 +534,12 @@
 
     lax.fori_loop(3, 7, side_windows, 0)
 
-    def outer_products(n, carry):
-        x = n // 3
-        dx = halo_shift(x, n % 3)
-        for y in range(B):
-            for dy in range(7):
-                multiply(x, dx, y, dy)
-        return carry
-
-    lax.fori_loop(0, 12, outer_products, 0)
-
-    def side_products(n, carry):
-        x = n // 4
-        dx = 3 - x + n % 4
-        for y in range(B):
-            for t in range(3):
-                multiply(x, dx, y, halo_shift(y, t))
-        return carry
-
-    lax.fori_loop(0, 16, side_products, 0)
+    for dx in range(7):
+        for dy in range(7):
+            for x in range(B):
+                for y in range(B):
+                    if not is_own(x, dx, y, dy):
+                        products(lhs[lhs_at(x, dx, y, dy, 0)], x, dx, y, dy)
     local = jnp.dot(lhs[...], wl[...], preferred_element_type=F32)
 
     lane_z = iota((4, 256), 1) // RANK
@@ -605,7 +581,7 @@
     operands = (coords, charges, order, near_list, far_list, coarse_list, up, wl, wp, down)
     return pl.pallas_call(
         functools.partial(main_kernel, count_g, count_d, log_y),
-        out_shape=jax.ShapeDtypeStruct((RHS, B, B, WIDTH), F32),
+        out_shape=pltpu.VMEM((RHS, B, B, WIDTH), F32),
         in_specs=[pl.BlockSpec(memory_space=pl.ANY)] * len(operands),
         out_specs=pl.BlockSpec(memory_space=pltpu.VMEM),
         scratch_shapes=[pltpu.VMEM(a.shape, a.dtype) for a in operands]
@@ -622,8 +598,7 @@
             pltpu.VMEM((10, 10, 2, 16, 256), BF),
             pltpu.VMEM((512, 49 * 256), BF),
             pltpu.VMEM((2, B, B, 16, 256), jnp.int32),
-            pltpu.VMEM((16, WIDTH, 32), BF),
-            pltpu.VMEM((16, 8, WIDTH), jnp.int32),
+            pltpu.VMEM((16, 9, 32, WIDTH), BF),
             pltpu.SemaphoreType.DMA((len(operands),)),
             pltpu.SemaphoreType.DMA((8, 3)),
             pltpu.SemaphoreType.DMA((8, 3)),

time: 37.2 us -> 26.2 us (0.70)
  the two profiles are of different devices: /device:TPU:24 before, /device:TPU:1 now
where the time goes in v2:
time: 26.2 us; the launch traced here: 26.1 us
  Pallas kernels  25.5 us (97%)
  local copies, waits for them, and re-layouts  0.63 us (2%)
    pallas_call x1, Pallas kernels, on_device(): pl.pallas_call(functools.partial(main_kernel, count_g, count_d, log_y), o...  25.5 us
    unnamed x1, local copies, waits for them, and re-layouts  0.63 us

profile of v2, /device:TPU:1, one launch (start us, length us, event | category | flops | bytes accessed | tf_op | source)
XLA Modules:
  0.0 26.1 jit_solution(13905267362961272255)
XLA Ops:
  0.0 25.5 %fields.1 = f32[8,4,4,128]{3,2,1,0:T(4,128)S(1)} custom-call(f32[3,4,4,128]{3,2,1,0:T(4,128)} %coords_in.1, f32[8,4,4,128]{3,2,1,0:T(4,128)} %charges_in.1, s32[4,4,128]{2,1,0:T(4,128)} %order_in.1, s32[4,4,4,27]{3,2,1,0:T(4,128)} %bitcast.4, s32[4,4,4,138]{3,2,1,0:T(4,128)} %bitcast.3, s32[2,2,2,32]{3,2,1,0:T(2,128)} %bitcast.5, ...), custom_call_target="tpu_custom_call" | custom-call | tf_op jit(solution)/shard_map/fields/pallas_call | solution.py:582
  25.5 0.6 %copy.12 = f32[8,4,4,128]{3,2,1,0:T(4,128)} copy(f32[8,4,4,128]{3,2,1,0:T(4,128)S(1)} %fields.1) | data formatting | bytes 131072

commit v3 on v2

--- a/solution.py
+++ b/solution.py
@@ -333,7 +333,7 @@
         s2 = jnp.where(row8 < 2, 1.0, own_box)
         return jnp.concatenate([s0, s1, s2, zeros8], axis=0).astype(BF), charge
 
-    def near_sums(sources, depth=1, width=4):
+    def near_sums(sources, depth=2, width=4):
         groups = []
         for (x, y), features in sources.items():
             near = [
@@ -377,24 +377,19 @@
     def window(x, y, tile):
         for half in range(2):
             m = tile[8 * half : 8 * half + 8].astype(F32)
-            turned = jnp.concatenate([m[4:8], m[0:4]], axis=0)
-            first = jnp.where(row8 < 4, m, turned)
-            last = jnp.where(row8 < 4, turned, m)
-            lanes = slice(128 * half, 128 * half + 128)
-            win[x, y, 0, :, lanes] = jnp.concatenate([first, first], axis=0).astype(BF)
-            win[x, y, 1, :, lanes] = jnp.concatenate([last, last], axis=0).astype(BF)
-
-    def lhs_at(x, dx, y, dy, s):
-        row = x * 128 + y * 32 + 16 * s
-        lane = dx * 1792 + 256 * dy
-        return slice(row, row + 16), slice(lane, lane + 256)
+            win[x, y, :, 128 * half : 128 * half + 128] = jnp.concatenate([m, m], axis=0).astype(BF)
 
     def is_own(x, dx, y, dy):
         return 3 <= x + dx < 7 and 3 <= y + dy < 7
 
-    def products(keep, x, dx, y, dy):
-        for s in range(2):
-            lhs[lhs_at(x, dx, y, dy, s)] = keep * win[x + dx, y + dy, s]
+    none = jnp.zeros((16, 256), BF)
+
+    def products(x, dx, y, dy):
+        slot = 7 * dx + dy
+        for zp in range(2):
+            row, lane = 256 * zp + 16 * (x * B + y), 256 * slot
+            keep = (words[slot // 13, x, y, zp] & jnp.int16(1 << (slot % 13))) != jnp.int16(0)
+            lhs[row : row + 16, lane : lane + 256] = jnp.where(keep, win[x + dx, y + dy], none)
 
     for load in loads[4:9]:
         load.wait()
@@ -404,10 +399,10 @@
             entries = far_list[x, y]
             ox, oy, zs = decode(entries, log_y, B * g + x, B * d + y, 3, 2)
             slot = 7 * ox + oy
-            late = slot >= 25
-            bit = one_bit(entries, jnp.where(late, slot - 25, slot))
-            for h in range(2):
-                mine = jnp.where(late == (h == 1), bit, 0)
+            part = jnp.where(slot >= 26, jnp.where(slot >= 39, 3, 2), jnp.where(slot >= 13, 1, 0))
+            bit = one_bit(entries, slot - 13 * part)
+            for h in range(4):
+                mine = jnp.where(part == h, bit, 0)
                 w = [jnp.sum(jnp.where(zs == z, mine, 0), axis=1, keepdims=True) for z in range(B)]
                 for half in range(2):
                     pair = jnp.where(
@@ -415,10 +410,13 @@
                         jnp.broadcast_to(w[2 * half], (4, 128)),
                         jnp.broadcast_to(w[2 * half + 1], (4, 128)),
                     )
-                    wide = jnp.broadcast_to(pair[0:1], (16, 128))
-                    for z in range(1, B):
-                        wide = jnp.where(row16 >= 4 * z, jnp.broadcast_to(pair[z : z + 1], (16, 128)), wide)
-                    words[h, x, y, :, 128 * half : 128 * half + 128] = wide
+                    for zp in range(2):
+                        wide = jnp.where(
+                            row16 < 8,
+                            jnp.broadcast_to(pair[2 * zp : 2 * zp + 1], (16, 128)),
+                            jnp.broadcast_to(pair[2 * zp + 1 : 2 * zp + 2], (16, 128)),
+                        )
+                        words[h, x, y, zp, :, 128 * half : 128 * half + 128] = wide.astype(jnp.int16)
         return carry
 
     lax.fori_loop(0, B, far_words, 0)
@@ -432,15 +430,9 @@
 
     for x in range(B):
         for y in range(B):
-            for h, first, last in ((0, 0, 25), (1, 25, 49)):
-                w = words[h, x, y]
-                for slot in range(first, last):
-                    dx, dy = slot // 7, slot % 7
-                    keep = jnp.where((w & (1 << (slot - first))) != 0, 1.0, 0.0).astype(BF)
-                    if is_own(x, dx, y, dy):
-                        products(keep, x, dx, y, dy)
-                    else:
-                        lhs[lhs_at(x, dx, y, dy, 0)] = keep
+            for dx in range(3 - x, 7 - x):
+                for dy in range(3 - y, 7 - y):
+                    products(x, dx, y, dy)
 
     own_source = {}
     for c in range(16):
@@ -539,22 +531,20 @@
             for x in range(B):
                 for y in range(B):
                     if not is_own(x, dx, y, dy):
-                        products(lhs[lhs_at(x, dx, y, dy, 0)], x, dx, y, dy)
-    local = jnp.dot(lhs[...], wl[...], preferred_element_type=F32)
-
-    lane_z = iota((4, 256), 1) // RANK
+                        products(x, dx, y, dy)
+    local = [
+        jnp.dot(
+            lhs[256 * zp : 256 * zp + 256, :], wl[:, 128 * zp : 128 * zp + 128], preferred_element_type=F32
+        )
+        for zp in range(2)
+    ]
+
     for c in range(16):
         x, y = c // B, c % B
-        halves = []
-        for s in range(2):
-            block = local[c * 32 + 16 * s : c * 32 + 16 * s + 16]
-            got = block[0:4]
-            for z in range(1, B):
-                got = jnp.where(lane_z == z, block[4 * z : 4 * z + 4], got)
-            halves.append(got)
+        halves = [jnp.where(lane8 < 64, v[16 * c : 16 * c + 8], v[16 * c + 8 : 16 * c + 16]) for v in local]
         q = (x // 2) * 2 + y // 2
         k = (x % 2) * 2 + y % 2
-        total = jnp.concatenate(halves, axis=0) + descent[8 * q : 8 * q + 8, 256 * k : 256 * k + 256]
+        total = jnp.concatenate(halves, axis=1) + descent[8 * q : 8 * q + 8, 256 * k : 256 * k + 256]
         far = jnp.dot(total.astype(BF), basis[c], preferred_element_type=F32)
         out_ref[:, x, y, :] = NUGGET * cs[c] + near_out[c] + far
     for copy in near_copies + moment_copies + parent_copies:
@@ -595,9 +585,9 @@
             pltpu.VMEM((6, 6, 16, WIDTH), BF),
             pltpu.VMEM((10, 10, 16, 128), BF),
             pltpu.VMEM((6, 3, 16, 128), BF),
-            pltpu.VMEM((10, 10, 2, 16, 256), BF),
+            pltpu.VMEM((10, 10, 16, 256), BF),
             pltpu.VMEM((512, 49 * 256), BF),
-            pltpu.VMEM((2, B, B, 16, 256), jnp.int32),
+            pltpu.VMEM((4, B, B, 2, 16, 256), jnp.int16),
             pltpu.VMEM((16, 9, 32, WIDTH), BF),
             pltpu.SemaphoreType.DMA((len(operands),)),
             pltpu.SemaphoreType.DMA((8, 3)),

time: 26.2 us -> 25.9 us (0.989)
  Pallas kernels: 25.5 us -> 25.1 us
    pallas_call x1, Pallas kernels: 25.5 us -> 25.1 us  [on_device(): pl.pallas_call(functools.partial(main_kernel, count_g, count_d, log_y), o...]
where the time goes in v3:
time: 25.9 us; the launch traced here: 25.8 us
  Pallas kernels  25.1 us (97%)
  local copies, waits for them, and re-layouts  0.63 us (2%)
    pallas_call x1, Pallas kernels, on_device(): pl.pallas_call(functools.partial(main_kernel, count_g, count_d, log_y), o...  25.1 us
    unnamed x1, local copies, waits for them, and re-layouts  0.63 us

profile of v3, /device:TPU:1, one launch (start us, length us, event | category | flops | bytes accessed | tf_op | source)
XLA Modules:
  0.0 25.8 jit_solution(9376909049000858384)
XLA Ops:
  0.0 25.1 %fields.1 = f32[8,4,4,128]{3,2,1,0:T(4,128)S(1)} custom-call(f32[3,4,4,128]{3,2,1,0:T(4,128)} %coords_in.1, f32[8,4,4,128]{3,2,1,0:T(4,128)} %charges_in.1, s32[4,4,128]{2,1,0:T(4,128)} %order_in.1, s32[4,4,4,27]{3,2,1,0:T(4,128)} %bitcast.4, s32[4,4,4,138]{3,2,1,0:T(4,128)} %bitcast.3, s32[2,2,2,32]{3,2,1,0:T(2,128)} %bitcast.5, ...), custom_call_target="tpu_custom_call" | custom-call | tf_op jit(solution)/shard_map/fields/pallas_call | solution.py:572
  25.1 0.6 %copy.12 = f32[8,4,4,128]{3,2,1,0:T(4,128)} copy(f32[8,4,4,128]{3,2,1,0:T(4,128)S(1)} %fields.1) | data formatting | bytes 131072
